TPU v7x, 256 devices: a whole 4x4x8 slice. The times are simulated.
256 devices in a mesh: qa: 16 (over z_lo, y), qb: 16 (over z_hi, x, core).
Axes of the slice: x: 4, y: 4, z: 8 (z_hi: 2, z_lo: 4; z = z_hi * 4 + z_lo), core: 2. Of those that a mesh axis runs over, the one named last changes fastest.
Arguments:
- amplitudes: float32 [16, 16, 1048576], P('qa', 'qb'), may hold values from -6 to 6
- gates: float32 [3, 2, 128, 128], replicated, may hold values from -0.5 to 0.5
- cz_pairs: int32 [3, 20, 2], replicated, may hold values from 0 to 19, as said below
Outputs:
- final_state: float32 [16, 16, 1048576], P('qa', 'qb')
Inputs may be any that keep to these rules, and one draw needn't show every extreme that they name: `cz_pairs`: in each layer the first qubits of the 20 pairs are all different, and the two qubits of a pair differ.
All inputs are finite; a program needn't handle non-finite values.
Results may differ from a plain program's by a relative error of at most 0.0001.
Values sent between devices are 32-bit elements; how exact they have to be, the bound alone decides.
No kernel may reach another device: no remote copies, remote signals or barrier semaphores. Data moves between devices by JAX's collectives and lax.ppermute only.
A program may use at most 64 MiB of HBM per device.

v0:
```python
import jax
import jax.numpy as jnp
from jax import lax
from jax.sharding import PartitionSpec as P

LAYERS = 3


def from_partner(value, axis, distance):
    mask = 2**distance
    pairs = [(source, source ^ mask) for source in range(lax.axis_size(axis))]
    return lax.ppermute(value, axis, pairs)


def cz_sign(positions, pair_list):
    parity = jnp.zeros(positions.shape, jnp.int32)
    for pair_idx in range(pair_list.shape[0]):
        first_bit = jnp.right_shift(positions, pair_list[pair_idx, 0]) & 1
        second_bit = jnp.right_shift(positions, pair_list[pair_idx, 1]) & 1
        parity = parity + first_bit * second_bit
    return 1.0 - 2.0 * (parity % 2).astype(jnp.float32)


def swap_qa_bits(vector):
    lead_rows, side_len, last_len = vector.shape
    count = lax.axis_size("qa")
    for bit_pos in range(count.bit_length() - 1):
        upper = count >> bit_pos + 1
        shaped = vector.reshape(lead_rows, upper, 2, side_len // (upper * 2), last_len)
        my_bit = jnp.right_shift(lax.axis_index("qa"), bit_pos) & 1
        kept_half = lax.dynamic_index_in_dim(shaped, my_bit, 2, keepdims=True)
        sent_half = lax.dynamic_index_in_dim(shaped, 1 - my_bit, 2, keepdims=True)
        received = from_partner(sent_half, "qa", bit_pos)
        low_first = jnp.concatenate([kept_half, received], 2)
        high_first = jnp.concatenate([received, kept_half], 2)
        vector = jnp.where(my_bit == 0, low_first, high_first).reshape(
            lead_rows, side_len, last_len
        )
    return vector


def swap_qb_bits(vector):
    lead_rows, side_len, last_len = vector.shape
    count = lax.axis_size("qb")
    for bit_pos in range(count.bit_length() - 1):
        upper = count >> bit_pos + 1
        shaped = vector.reshape(lead_rows, side_len, upper, 2, last_len // (upper * 2))
        my_bit = jnp.right_shift(lax.axis_index("qb"), bit_pos) & 1
        kept_half = lax.dynamic_index_in_dim(shaped, my_bit, 3, keepdims=True)
        sent_half = lax.dynamic_index_in_dim(shaped, 1 - my_bit, 3, keepdims=True)
        received = from_partner(sent_half, "qb", bit_pos)
        low_first = jnp.concatenate([kept_half, received], 3)
        high_first = jnp.concatenate([received, kept_half], 3)
        vector = jnp.where(my_bit == 0, low_first, high_first).reshape(
            lead_rows, side_len, last_len
        )
    return vector


def per_device(amplitudes, gates, cz_pairs):
    total_amp = amplitudes.shape[2]
    side_len = gates.shape[-1]
    lead_rows = total_amp // (side_len * side_len)
    vector = amplitudes.reshape(lead_rows, side_len, side_len)
    shape_three = (lead_rows, side_len, side_len)
    positions = (
        lax.broadcasted_iota(jnp.int32, shape_three, 0) * (side_len * side_len)
        + lax.broadcasted_iota(jnp.int32, shape_three, 1) * side_len
        + lax.broadcasted_iota(jnp.int32, shape_three, 2)
    )
    for layer_idx in range(LAYERS):
        vector = jnp.einsum(
            "xyk,ik->xyi", vector, gates[layer_idx, 0], precision=lax.Precision.HIGHEST
        )
        vector = jnp.einsum(
            "xky,ik->xiy", vector, gates[layer_idx, 1], precision=lax.Precision.HIGHEST
        )
        vector = vector * cz_sign(positions, cz_pairs[layer_idx])
        if layer_idx + 1 < LAYERS:
            vector = swap_qb_bits(swap_qa_bits(vector))
    return vector.reshape(1, 1, total_amp)


def solution(mesh):
    in_specs = (P("qa", "qb", None), P(), P())
    out_specs = P("qa", "qb", None)
    return jax.shard_map(
        per_device, mesh=mesh, in_specs=in_specs, out_specs=out_specs, check_vma=False
    )
```

profile of v0, /device:TPU:1, one launch (start us, length us, event | category | flops | bytes accessed | tf_op | source)
XLA Modules:
  0.0 1111.7 jit_solution(1309691861023125791)
XLA Ops:
  2.8 6.6 fusion.22
  9.4 48.4 %fusion.4 = f32[64,128,128]{2,1,0:T(8,128)S(1)} fusion(f32[64,128,128]{2,1,0:T(8,128)} %fusion.22, s32[]{:T(128)} %bitcast.46, s32[]{:T(128)} %bitcast.45, s32[]{:T(128)} %bitcast.44, s32[]{:T(128)} %bitcast.43, s32[]{:T(128)} %bitcast.42, s32[]{:T(128)} %bitcast.41, s32[]{:T(128)} %bitcast.40, s32[]{:T(128)} %bitcast.39, s32[]{:T(128)} %bitcast.38, ...), kind=kOutput, calls=%fused_computation.13 | convolution fusion | flops 1753219072 | bytes 8455328 | tf_op jit(solution)/shard_map/xky,ik->xiy/dot_general | solution.py:75
  61.5 44.4 %collective-permute-done = f32[64,8,1,8,128]{4,3,2,1,0:T(8,128)} collective-permute-done((f32[64,8,1,8,128]{4,3,2,1,0:T(8,128)}, f32[64,8,1,8,128]{4,3,2,1,0:T(8,128)}, u32[]{:S(2)}, u32[]{:S(2)}) %collective-permute-start) | collective-permute-done | bytes 2097184 | tf_op jit(solution)/shard_map/ppermute | solution.py:12
  110.7 4.2 collective-permute-start.1
  114.9 44.6 %collective-permute-done.1 = f32[64,4,1,16,128]{4,3,2,1,0:T(8,128)} collective-permute-done((f32[64,4,1,16,128]{4,3,2,1,0:T(8,128)}, f32[64,4,1,16,128]{4,3,2,1,0:T(8,128)}, u32[]{:S(2)}, u32[]{:S(2)}) %collective-permute-start.1) | collective-permute-done | bytes 2097184 | tf_op jit(solution)/shard_map/ppermute | solution.py:12
  165.8 43.7 %collective-permute-done.2 = f32[64,2,1,32,128]{4,3,2,1,0:T(8,128)} collective-permute-done((f32[64,2,1,32,128]{4,3,2,1,0:T(8,128)}, f32[64,2,1,32,128]{4,3,2,1,0:T(8,128)}, u32[]{:S(2)}, u32[]{:S(2)}) %collective-permute-start.2) | collective-permute-done | bytes 2097184 | tf_op jit(solution)/shard_map/ppermute | solution.py:12
  217.1 90.3 %collective-permute-done.3 = f32[64,1,1,64,128]{4,3,2,0,1:T(8,128)} collective-permute-done((f32[64,1,1,64,128]{4,3,2,0,1:T(8,128)}, f32[64,1,1,64,128]{4,3,2,0,1:T(8,128)}, u32[]{:S(2)}, u32[]{:S(2)}) %collective-permute-start.3) | collective-permute-done | bytes 2097184 | tf_op jit(solution)/shard_map/ppermute | solution.py:12
  307.3 5.1 maximum_select_fusion.3
  312.5 10.9 copy.8
  323.3 8.8 select_n.327
  332.1 4.0 constant_dynamic-slice_fusion.23
  337.7 4.1 collective-permute-done.4
  347.8 46.0 %collective-permute-done.5 = f32[64,128,4,1,16]{1,4,3,2,0:T(8,128)} collective-permute-done((f32[64,128,4,1,16]{1,4,3,2,0:T(8,128)}, f32[64,128,4,1,16]{1,4,3,2,0:T(8,128)}, u32[]{:S(2)}, u32[]{:S(2)}) %collective-permute-start.5) | collective-permute-done | bytes 2097184 | tf_op jit(solution)/shard_map/ppermute | solution.py:12
  401.3 45.0 %collective-permute-done.6 = f32[64,128,2,1,32]{1,4,3,2,0:T(8,128)} collective-permute-done((f32[64,128,2,1,32]{1,4,3,2,0:T(8,128)}, f32[64,128,2,1,32]{1,4,3,2,0:T(8,128)}, u32[]{:S(2)}, u32[]{:S(2)}) %collective-permute-start.6) | collective-permute-done | bytes 2097184 | tf_op jit(solution)/shard_map/ppermute | solution.py:12
  450.9 6.3 collective-permute-start.7
  459.3 87.5 %collective-permute-done.7 = f32[64,128,1,1,64]{1,4,3,2,0:T(8,128)} collective-permute-done((f32[64,128,1,1,64]{1,4,3,2,0:T(8,128)}, f32[64,128,1,1,64]{1,4,3,2,0:T(8,128)}, u32[]{:S(2)}, u32[]{:S(2)}) %collective-permute-start.7) | collective-permute-done | bytes 2097184 | tf_op jit(solution)/shard_map/ppermute | solution.py:12
  549.7 6.7 fusion.19
  556.4 46.9 %fusion.9 = f32[64,128,128]{2,1,0:T(8,128)S(1)} fusion(f32[64,128,128]{2,1,0:T(8,128)S(1)} %fusion.19, s32[]{:T(128)} %bitcast.100, s32[]{:T(128)} %bitcast.99, s32[]{:T(128)} %bitcast.98, s32[]{:T(128)} %bitcast.97, s32[]{:T(128)} %bitcast.96, s32[]{:T(128)} %bitcast.95, s32[]{:T(128)} %bitcast.94, s32[]{:T(128)} %bitcast.93, s32[]{:T(128)} %bitcast.92, ...), kind=kOutput, calls=%fused_computation.18 | convolution fusion | flops 1753219072 | bytes 8455328 | tf_op jit(solution)/shard_map/xky,ik->xiy/dot_general | solution.py:75
  605.2 43.0 %collective-permute-done.8 = f32[64,8,1,8,128]{4,3,2,1,0:T(8,128)S(1)} collective-permute-done((f32[64,8,1,8,128]{4,3,2,1,0:T(8,128)S(1)}, f32[64,8,1,8,128]{4,3,2,1,0:T(8,128)S(1)}, u32[]{:S(2)}, u32[]{:S(2)}) %collective-permute-start.8) | collective-permute-done | bytes 2097184 | tf_op jit(solution)/shard_map/ppermute | solution.py:12
  652.6 42.3 %collective-permute-done.9 = f32[64,4,1,16,128]{4,3,2,1,0:T(8,128)S(1)} collective-permute-done((f32[64,4,1,16,128]{4,3,2,1,0:T(8,128)S(1)}, f32[64,4,1,16,128]{4,3,2,1,0:T(8,128)S(1)}, u32[]{:S(2)}, u32[]{:S(2)}) %collective-permute-start.9) | collective-permute-done | bytes 2097184 | tf_op jit(solution)/shard_map/ppermute | solution.py:12
  696.0 42.6 %collective-permute-done.10 = f32[64,2,1,32,128]{4,3,2,1,0:T(8,128)S(1)} collective-permute-done((f32[64,2,1,32,128]{4,3,2,1,0:T(8,128)S(1)}, f32[64,2,1,32,128]{4,3,2,1,0:T(8,128)S(1)}, u32[]{:S(2)}, u32[]{:S(2)}) %collective-permute-start.10) | collective-permute-done | bytes 2097184 | tf_op jit(solution)/shard_map/ppermute | solution.py:12
  739.8 5.0 collective-permute-start.11
  744.8 89.8 %collective-permute-done.11 = f32[64,1,1,64,128]{4,3,2,0,1:T(8,128)S(1)} collective-permute-done((f32[64,1,1,64,128]{4,3,2,0,1:T(8,128)S(1)}, f32[64,1,1,64,128]{4,3,2,0,1:T(8,128)S(1)}, u32[]{:S(2)}, u32[]{:S(2)}) %collective-permute-start.11) | collective-permute-done | bytes 2097184 | tf_op jit(solution)/shard_map/ppermute | solution.py:12
  837.1 10.9 copy.10
  847.9 8.8 select_n.352
  861.1 3.8 collective-permute-done.12
  867.6 45.5 %collective-permute-done.13 = f32[64,128,4,1,16]{1,4,3,2,0:T(8,128)S(1)} collective-permute-done((f32[64,128,4,1,16]{1,4,3,2,0:T(8,128)S(1)}, f32[64,128,4,1,16]{1,4,3,2,0:T(8,128)S(1)}, u32[]{:S(2)}, u32[]{:S(2)}) %collective-permute-start.13) | collective-permute-done | bytes 2097184 | tf_op jit(solution)/shard_map/ppermute | solution.py:12
  914.2 3.1 collective-permute-start.14
  917.3 44.7 %collective-permute-done.14 = f32[64,128,2,1,32]{1,4,3,2,0:T(8,128)S(1)} collective-permute-done((f32[64,128,2,1,32]{1,4,3,2,0:T(8,128)S(1)}, f32[64,128,2,1,32]{1,4,3,2,0:T(8,128)S(1)}, u32[]{:S(2)}, u32[]{:S(2)}) %collective-permute-start.14) | collective-permute-done | bytes 2097184 | tf_op jit(solution)/shard_map/ppermute | solution.py:12
  966.7 91.5 %collective-permute-done.15 = f32[64,128,1,1,64]{1,4,3,2,0:T(8,128)S(1)} collective-permute-done((f32[64,128,1,1,64]{1,4,3,2,0:T(8,128)S(1)}, f32[64,128,1,1,64]{1,4,3,2,0:T(8,128)S(1)}, u32[]{:S(2)}, u32[]{:S(2)}) %collective-permute-start.15) | collective-permute-done | bytes 2097184 | tf_op jit(solution)/shard_map/ppermute | solution.py:12
  1059.0 4.2 fusion.16
  1063.2 48.1 %fusion.14 = f32[64,128,128]{2,1,0:T(8,128)} fusion(f32[64,128,128]{1,2,0:T(8,128)S(1)} %fusion.16, s32[]{:T(128)} %bitcast.154, s32[]{:T(128)} %bitcast.153, s32[]{:T(128)} %bitcast.152, s32[]{:T(128)} %bitcast.151, s32[]{:T(128)} %bitcast.150, s32[]{:T(128)} %bitcast.149, s32[]{:T(128)} %bitcast.148, s32[]{:T(128)} %bitcast.147, s32[]{:T(128)} %bitcast.146, ...), kind=kOutput, calls=%fused_computation.23 | convolution fusion | flops 1753219072 | bytes 8455328 | tf_op jit(solution)/shard_map/xky,ik->xiy/dot_general | solution.py:75
  (55 shorter events, 74.5 us)
Async XLA Ops:
  2.8 6.6 copy-start
  59.4 46.6 %collective-permute-start = (f32[64,8,1,8,128]{4,3,2,1,0:T(8,128)}, f32[64,8,1,8,128]{4,3,2,1,0:T(8,128)}, u32[]{:S(2)}, u32[]{:S(2)}) collective-permute-start(f32[64,8,1,8,128]{4,3,2,1,0:T(8,128)} %get-tuple-element.36), channel_id=1, source_target_pairs={{0,16},{16,0},{32,48},{48,32},{64,80},{80,64},{96,112},{112,96},{1... | collective-permute-start | bytes 6291464 | tf_op jit(solution)/shard_map/ppermute | solution.py:12
  110.7 48.7 %collective-permute-start.1 = (f32[64,4,1,16,128]{4,3,2,1,0:T(8,128)}, f32[64,4,1,16,128]{4,3,2,1,0:T(8,128)}, u32[]{:S(2)}, u32[]{:S(2)}) collective-permute-start(f32[64,4,1,16,128]{4,3,2,1,0:T(8,128)} %get-tuple-element.34), channel_id=1, source_target_pairs={{0,32},{16,48},{32,0},{48,16},{64,96},{80,112},{96,64},{112,80},{1... | collective-permute-start | bytes 6291464 | tf_op jit(solution)/shard_map/ppermute | solution.py:12
  164.2 45.3 %collective-permute-start.2 = (f32[64,2,1,32,128]{4,3,2,1,0:T(8,128)}, f32[64,2,1,32,128]{4,3,2,1,0:T(8,128)}, u32[]{:S(2)}, u32[]{:S(2)}) collective-permute-start(f32[64,2,1,32,128]{4,3,2,1,0:T(8,128)} %get-tuple-element.32), channel_id=1, source_target_pairs={{0,64},{16,80},{32,96},{48,112},{64,0},{80,16},{96,32},{112,48},{1... | collective-permute-start | bytes 6291464 | tf_op jit(solution)/shard_map/ppermute | solution.py:12
  214.1 93.2 %collective-permute-start.3 = (f32[64,1,1,64,128]{4,3,2,0,1:T(8,128)}, f32[64,1,1,64,128]{4,3,2,0,1:T(8,128)}, u32[]{:S(2)}, u32[]{:S(2)}) collective-permute-start(f32[64,1,1,64,128]{4,3,2,0,1:T(8,128)} %get-tuple-element.30), channel_id=1, source_target_pairs={{0,128},{16,144},{32,160},{48,176},{64,192},{80,208},{96,224},{112... | collective-permute-start | bytes 6291464 | tf_op jit(solution)/shard_map/ppermute | solution.py:12
  336.2 5.7 collective-permute-start.4
  346.6 47.2 %collective-permute-start.5 = (f32[64,128,4,1,16]{1,4,3,2,0:T(8,128)}, f32[64,128,4,1,16]{1,4,3,2,0:T(8,128)}, u32[]{:S(2)}, u32[]{:S(2)}) collective-permute-start(f32[64,128,4,1,16]{1,4,3,2,0:T(8,128)} %get-tuple-element.26), channel_id=1, source_target_pairs={{0,2},{1,3},{2,0},{3,1},{4,6},{5,7},{6,4},{7,5},{8,10},{9,11},{10,... | collective-permute-start | bytes 6291464 | tf_op jit(solution)/shard_map/ppermute | solution.py:12
  398.5 47.7 %collective-permute-start.6 = (f32[64,128,2,1,32]{1,4,3,2,0:T(8,128)}, f32[64,128,2,1,32]{1,4,3,2,0:T(8,128)}, u32[]{:S(2)}, u32[]{:S(2)}) collective-permute-start(f32[64,128,2,1,32]{1,4,3,2,0:T(8,128)} %get-tuple-element.24), channel_id=1, source_target_pairs={{0,4},{1,5},{2,6},{3,7},{4,0},{5,1},{6,2},{7,3},{8,12},{9,13},{10,... | collective-permute-start | bytes 6291464 | tf_op jit(solution)/shard_map/ppermute | solution.py:12
  450.9 95.9 %collective-permute-start.7 = (f32[64,128,1,1,64]{1,4,3,2,0:T(8,128)}, f32[64,128,1,1,64]{1,4,3,2,0:T(8,128)}, u32[]{:S(2)}, u32[]{:S(2)}) collective-permute-start(f32[64,128,1,1,64]{1,4,3,2,0:T(8,128)} %get-tuple-element.22), channel_id=1, source_target_pairs={{0,8},{1,9},{2,10},{3,11},{4,12},{5,13},{6,14},{7,15},{8,0},{9,1},... | collective-permute-start | bytes 6291464 | tf_op jit(solution)/shard_map/ppermute | solution.py:12
  603.6 44.6 %collective-permute-start.8 = (f32[64,8,1,8,128]{4,3,2,1,0:T(8,128)S(1)}, f32[64,8,1,8,128]{4,3,2,1,0:T(8,128)S(1)}, u32[]{:S(2)}, u32[]{:S(2)}) collective-permute-start(f32[64,8,1,8,128]{4,3,2,1,0:T(8,128)S(1)} %get-tuple-element.20), channel_id=1, source_target_pairs={{0,16},{16,0},{32,48},{48,32},{64,80},{80,64},{96,112},{112,96},{1... | collective-permute-start | bytes 6291464 | tf_op jit(solution)/shard_map/ppermute | solution.py:12
  649.6 45.3 %collective-permute-start.9 = (f32[64,4,1,16,128]{4,3,2,1,0:T(8,128)S(1)}, f32[64,4,1,16,128]{4,3,2,1,0:T(8,128)S(1)}, u32[]{:S(2)}, u32[]{:S(2)}) collective-permute-start(f32[64,4,1,16,128]{4,3,2,1,0:T(8,128)S(1)} %get-tuple-element.18), channel_id=1, source_target_pairs={{0,32},{16,48},{32,0},{48,16},{64,96},{80,112},{96,64},{112,80},{1... | collective-permute-start | bytes 6291464 | tf_op jit(solution)/shard_map/ppermute | solution.py:12
  695.9 42.7 %collective-permute-start.10 = (f32[64,2,1,32,128]{4,3,2,1,0:T(8,128)S(1)}, f32[64,2,1,32,128]{4,3,2,1,0:T(8,128)S(1)}, u32[]{:S(2)}, u32[]{:S(2)}) collective-permute-start(f32[64,2,1,32,128]{4,3,2,1,0:T(8,128)S(1)} %get-tuple-element.16), channel_id=1, source_target_pairs={{0,64},{16,80},{32,96},{48,112},{64,0},{80,16},{96,32},{112,48},{1... | collective-permute-start | bytes 6291464 | tf_op jit(solution)/shard_map/ppermute | solution.py:12
  739.8 94.8 %collective-permute-start.11 = (f32[64,1,1,64,128]{4,3,2,0,1:T(8,128)S(1)}, f32[64,1,1,64,128]{4,3,2,0,1:T(8,128)S(1)}, u32[]{:S(2)}, u32[]{:S(2)}) collective-permute-start(f32[64,1,1,64,128]{4,3,2,0,1:T(8,128)S(1)} %get-tuple-element.14), channel_id=1, source_target_pairs={{0,128},{16,144},{32,160},{48,176},{64,192},{80,208},{96,224},{112... | collective-permute-start | bytes 6291464 | tf_op jit(solution)/shard_map/ppermute | solution.py:12
  859.3 5.6 collective-permute-start.12
  866.2 46.9 %collective-permute-start.13 = (f32[64,128,4,1,16]{1,4,3,2,0:T(8,128)S(1)}, f32[64,128,4,1,16]{1,4,3,2,0:T(8,128)S(1)}, u32[]{:S(2)}, u32[]{:S(2)}) collective-permute-start(f32[64,128,4,1,16]{1,4,3,2,0:T(8,128)S(1)} %get-tuple-element.10), channel_id=1, source_target_pairs={{0,2},{1,3},{2,0},{3,1},{4,6},{5,7},{6,4},{7,5},{8,10},{9,11},{10,... | collective-permute-start | bytes 6291464 | tf_op jit(solution)/shard_map/ppermute | solution.py:12
  914.2 47.8 %collective-permute-start.14 = (f32[64,128,2,1,32]{1,4,3,2,0:T(8,128)S(1)}, f32[64,128,2,1,32]{1,4,3,2,0:T(8,128)S(1)}, u32[]{:S(2)}, u32[]{:S(2)}) collective-permute-start(f32[64,128,2,1,32]{1,4,3,2,0:T(8,128)S(1)} %get-tuple-element.8), channel_id=1, source_target_pairs={{0,4},{1,5},{2,6},{3,7},{4,0},{5,1},{6,2},{7,3},{8,12},{9,13},{10,... | collective-permute-start | bytes 6291464 | tf_op jit(solution)/shard_map/ppermute | solution.py:12
  963.2 95.0 %collective-permute-start.15 = (f32[64,128,1,1,64]{1,4,3,2,0:T(8,128)S(1)}, f32[64,128,1,1,64]{1,4,3,2,0:T(8,128)S(1)}, u32[]{:S(2)}, u32[]{:S(2)}) collective-permute-start(f32[64,128,1,1,64]{1,4,3,2,0:T(8,128)S(1)} %get-tuple-element.6), channel_id=1, source_target_pairs={{0,8},{1,9},{2,10},{3,11},{4,12},{5,13},{6,14},{7,15},{8,0},{9,1},... | collective-permute-start | bytes 6291464 | tf_op jit(solution)/shard_map/ppermute | solution.py:12
where the time goes:
time: 1120 us; the launch traced here: 1110 us
  waiting for transfers between devices  809 us (72%)
  matrix products  161 us (14%)
  local copies, waits for them, and re-layouts  67.5 us (6%)
  starting transfers between devices  40.7 us (4%)
  other arithmetic  33.4 us (3%)
    ppermute x16, waiting for transfers between devices, from_partner(): return lax.ppermute(value, axis, pairs)  809 us
    dot_general x3, matrix products, per_device(): jnp.einsum('xky,ik->xiy', vector, gates[layer_idx, 1], precision=lax.Prec...  143 us
    ppermute x16, starting transfers between devices, from_partner(): return lax.ppermute(value, axis, pairs)  40.7 us
    select_n x4, local copies, waits for them, and re-layouts, swap_qa_bits(): jnp.where(my_bit == 0, low_first, high_first)  39.4 us
  transfers between devices with their start and end apart: 16, of which 16 were waited for; matrix products, arithmetic and copies ran while one was open for 0% of the time, Pallas kernels for 0%

commit v1 on v0

v1 whole, which is shorter than its diff:
```python
import functools

import jax
import jax.numpy as jnp
from jax import lax
from jax.experimental import pallas as pl
from jax.experimental.pallas import tpu as pltpu
from jax.sharding import PartitionSpec as P

LAYERS = 3
SIDE = 128
ROWS_STEP = 1024
AXES = ("qa", "qb")
VMEM = 48 * 1024 * 1024


def split(value):
    high = value.astype(jnp.bfloat16)
    low = (value - high.astype(jnp.float32)).astype(jnp.bfloat16)
    return high, low


def gate_stack(gate):
    high, low = split(gate)
    return jnp.concatenate(
        [jnp.concatenate([high, high], 1), jnp.concatenate([low, low], 1)], 0
    )


def apply_rows(stack, value):
    high, low = split(value)
    both = jnp.dot(
        stack, jnp.concatenate([high, low], 0), preferred_element_type=jnp.float32
    )
    return both[:SIDE] + both[SIDE:]


def apply_lanes(stack, value):
    high, low = split(value)
    both = lax.dot_general(
        jnp.concatenate([high, low], 1),
        stack,
        (((1,), (1,)), ((), ())),
        preferred_element_type=jnp.float32,
    )
    return both[:, :SIDE] + both[:, SIDE:]


def sign_of(positions, pairs_ref, layer):
    parity = jnp.zeros(positions.shape, jnp.int32)
    for pair in range(pairs_ref.shape[1]):
        first = jnp.right_shift(positions, pairs_ref[layer, pair, 0])
        second = jnp.right_shift(positions, pairs_ref[layer, pair, 1])
        parity = parity ^ (first & second)
    return 1.0 - 2.0 * (parity & 1).astype(jnp.float32)


def fold_parity(value):
    for shift in (8, 4, 2, 1):
        value = value ^ jnp.right_shift(value, shift)
    return value & 1


def native_kernel(layer, slot, pairs_ref, masks_ref, gates_ref, in_ref, out_ref, stacks, table):
    step = pl.program_id(0)

    @pl.when(step == 0)
    def _():
        stacks[0] = gate_stack(gates_ref[layer, 0])
        stacks[1] = gate_stack(gates_ref[layer, 1])
        rows = lax.broadcasted_iota(jnp.int32, (SIDE, SIDE), 0)
        lanes = lax.broadcasted_iota(jnp.int32, (SIDE, SIDE), 1)
        table[...] = sign_of(rows * SIDE + lanes, pairs_ref, layer)

    low_bits = lax.broadcasted_iota(jnp.int32, (8, SIDE), 0) * SIDE + (
        lax.broadcasted_iota(jnp.int32, (8, SIDE), 1)
    )
    stack_z = stacks[0]
    stack_y = stacks[1]
    x_step = ROWS_STEP // SIDE
    for pair in range(x_step // 2):
        base = pair * 2 * SIDE
        value = apply_lanes(stack_z, in_ref[base : base + 2 * SIDE])
        value = apply_rows(
            stack_y, jnp.concatenate([value[:SIDE], value[SIDE:]], 1)
        )
        for half in range(2):
            mask = masks_ref[slot, step * x_step + pair * 2 + half]
            parity = fold_parity((low_bits & mask) ^ (jnp.right_shift(mask, 14) & 1))
            signs = [1.0 - 2.0 * parity.astype(jnp.float32)]
            for bit in range(4):
                flip = jnp.right_shift(mask, 10 + bit) & 1
                factor = 1.0 - 2.0 * flip.astype(jnp.float32)
                signs = signs + [sign * factor for sign in signs]
            sign = jnp.concatenate(signs, 0) * table[...]
            start = base + half * SIDE
            out_ref[start : start + SIDE] = (
                value[:, half * SIDE : (half + 1) * SIDE] * sign
            )


def native_layer(layer, slot, pairs, masks, gates, state):
    steps = state.shape[0] // ROWS_STEP
    return pl.pallas_call(
        functools.partial(native_kernel, layer, slot),
        grid=(steps,),
        in_specs=[
            pl.BlockSpec(memory_space=pltpu.SMEM),
            pl.BlockSpec(memory_space=pltpu.SMEM),
            pl.BlockSpec(memory_space=pltpu.VMEM),
            pl.BlockSpec((ROWS_STEP, SIDE), lambda i: (i, 0)),
        ],
        out_specs=pl.BlockSpec((ROWS_STEP, SIDE), lambda i: (i, 0)),
        out_shape=jax.ShapeDtypeStruct(state.shape, jnp.float32),
        scratch_shapes=[
            pltpu.VMEM((2, 2 * SIDE, 2 * SIDE), jnp.bfloat16),
            pltpu.VMEM((SIDE, SIDE), jnp.float32),
        ],
        compiler_params=pltpu.CompilerParams(vmem_limit_bytes=VMEM),
        cost_estimate=pl.CostEstimate(
            flops=16 * state.size * SIDE, bytes_accessed=8 * state.size, transcendentals=0
        ),
    )(pairs, masks, gates, state)


def middle_kernel(layer, pairs_ref, x_ref, gates_ref, in_ref, out_ref, stacks, table, first, second):
    @pl.when(pl.program_id(0) == 0)
    def _():
        stacks[0] = gate_stack(gates_ref[layer, 0])
        stacks[1] = gate_stack(gates_ref[layer, 1])
        rows = lax.broadcasted_iota(jnp.int32, (SIDE, SIDE), 0)
        lanes = lax.broadcasted_iota(jnp.int32, (SIDE, SIDE), 1)
        positions = x_ref[0] * (SIDE * SIDE) + lanes * SIDE + rows
        table[...] = sign_of(positions, pairs_ref, layer)

    stack_z = stacks[0]
    stack_y = stacks[1]

    def square(ref, b):
        return ref[:, b].reshape(SIDE, SIDE)

    for b in range(0, 16, 2):
        value = jnp.concatenate([square(in_ref, b), square(in_ref, b + 1)], 1)
        value = apply_rows(stack_y, value)
        first[b] = value[:, :SIDE].T.reshape(16, 8, SIDE)
        first[b + 1] = value[:, SIDE:].T.reshape(16, 8, SIDE)
    for d in range(0, 16, 2):
        value = jnp.concatenate([square(first, d), square(first, d + 1)], 1)
        value = apply_rows(stack_z, value)
        second[d] = (value[:, :SIDE] * table[...]).reshape(16, 8, SIDE)
        second[d + 1] = (value[:, SIDE:] * table[...]).reshape(16, 8, SIDE)
    for b in range(16):
        out_ref[:, b] = square(second, b).T.reshape(16, 8, SIDE)


def middle_layer(layer, pairs, x_index, gates, state):
    n_qa, n_qb, rows, _ = state.shape
    block = (n_qa, n_qb, 8, SIDE)
    return pl.pallas_call(
        functools.partial(middle_kernel, layer),
        grid=(rows // 8,),
        in_specs=[
            pl.BlockSpec(memory_space=pltpu.SMEM),
            pl.BlockSpec(memory_space=pltpu.SMEM),
            pl.BlockSpec(memory_space=pltpu.VMEM),
            pl.BlockSpec(block, lambda i: (0, 0, i, 0)),
        ],
        out_specs=pl.BlockSpec(block, lambda i: (0, 0, i, 0)),
        out_shape=jax.ShapeDtypeStruct(state.shape, jnp.float32),
        scratch_shapes=[
            pltpu.VMEM((2, 2 * SIDE, 2 * SIDE), jnp.bfloat16),
            pltpu.VMEM((SIDE, SIDE), jnp.float32),
            pltpu.VMEM((n_qb, 16, 8, SIDE), jnp.float32),
            pltpu.VMEM((16, n_qb, 8, SIDE), jnp.float32),
        ],
        compiler_params=pltpu.CompilerParams(vmem_limit_bytes=VMEM),
        cost_estimate=pl.CostEstimate(
            flops=16 * state.size * SIDE, bytes_accessed=8 * state.size, transcendentals=0
        ),
    )(pairs, x_index, gates, state)


def x_masks(pairs, count):
    x = jnp.arange(count, dtype=jnp.int32)[None]
    mask = jnp.zeros((2, count), jnp.int32)
    for pair in range(pairs.shape[1]):
        p = pairs[::2, pair, 0][:, None]
        q = pairs[::2, pair, 1][:, None]
        bit_p = jnp.where(p >= 14, jnp.right_shift(x, jnp.maximum(p - 14, 0)) & 1, 0)
        bit_q = jnp.where(q >= 14, jnp.right_shift(x, jnp.maximum(q - 14, 0)) & 1, 0)
        both = jnp.left_shift(bit_p & bit_q, 14)
        cross = jnp.where(
            q < 14,
            jnp.left_shift(bit_p, jnp.minimum(q, 14)),
            jnp.where(p < 14, jnp.left_shift(bit_q, jnp.minimum(p, 14)), both),
        )
        mask = mask ^ cross
    return mask


def per_device(amplitudes, gates, cz_pairs):
    total = amplitudes.shape[2]
    n_qa, n_qb = lax.axis_size("qa"), lax.axis_size("qb")
    state = amplitudes.reshape(total // SIDE, SIDE)
    masks = x_masks(cz_pairs, total // (SIDE * SIDE))
    device = lax.axis_index("qa") * n_qb + lax.axis_index("qb")
    x_index = jnp.right_shift(device, 2).astype(jnp.int32).reshape(1)
    blocks = n_qa * n_qb
    block_rows = total // SIDE // blocks
    state = native_layer(0, 0, cz_pairs, masks, gates, state)
    state = lax.all_to_all(state.reshape(blocks, block_rows, SIDE), AXES, 0, 0)
    state = state.reshape(n_qa, n_qb, block_rows, SIDE)
    state = middle_layer(1, cz_pairs, x_index, gates, state)
    state = lax.all_to_all(state.reshape(blocks, block_rows, SIDE), AXES, 0, 0)
    state = state.reshape(total // SIDE, SIDE)
    state = native_layer(2, 1, cz_pairs, masks, gates, state)
    return state.reshape(1, 1, total)


def solution(mesh):
    in_specs = (P("qa", "qb", None), P(), P())
    out_specs = P("qa", "qb", None)
    return jax.shard_map(
        per_device, mesh=mesh, in_specs=in_specs, out_specs=out_specs, check_vma=False
    )
```

time: 1120 us -> 265 us (0.24)
  waiting for transfers between devices: 809 us -> 96.3 us
  matrix products: 161 us -> 0 us
  blocking collectives: 0 us -> 105 us
  local copies, waits for them, and re-layouts: 67.5 us -> 3.79 us
  Pallas kernels: 0 us -> 24.8 us
  starting transfers between devices: 40.7 us -> 16.7 us
  other arithmetic: 33.4 us -> 17.7 us
    ppermute x16 -> x0, waiting for transfers between devices: 809 us -> none  [from_partner(): return lax.ppermute(value, axis, pairs)]
    dot_general x6 -> x0, matrix products: 161 us -> none  [the longest x3 143 us: per_device(): jnp.einsum('xky,ik->xiy', vector, gates[layer_idx, 1], precision=lax.Prec...]
    all_to_all x0 -> x1, blocking collectives: none -> 105 us  [per_device(): state = lax.all_to_all(state.reshape(blocks, block_rows, SIDE), AXES, 0, 0)]
    all_to_all x0 -> x1, waiting for transfers between devices: none -> 96.3 us  [per_device(): state = lax.all_to_all(state.reshape(blocks, block_rows, SIDE), AXES, 0, 0)]
    ppermute x16 -> x0, starting transfers between devices: 40.7 us -> none  [from_partner(): return lax.ppermute(value, axis, pairs)]
    select_n x4 -> x0, local copies, waits for them, and re-layouts: 39.4 us -> none  [swap_qa_bits(): jnp.where(my_bit == 0, low_first, high_first)]
    select_n x16 -> x0, other arithmetic: 33.4 us -> none  [the longest x8 18.6 us: swap_qa_bits(): jnp.where(my_bit == 0, low_first, high_first)]
    pallas_call x0 -> x3, Pallas kernels: none -> 24.8 us  [the longest x2 18.1 us: native_layer(): pl.pallas_call(functools.partial(native_kernel, layer, slot), grid=(steps...]
  transfers between devices with their start and end apart: 16 -> 1, of which waited for: 16 -> 1; matrix products, arithmetic and copies ran while one was open for 0% -> 0% of each run, Pallas kernels for 0% -> 0%
where the time goes in v1:
time: 265 us; the launch traced here: 264 us
  blocking collectives  105 us (40%)
  waiting for transfers between devices  96.3 us (36%)
  Pallas kernels  24.8 us (9%)
  other arithmetic  17.7 us (7%)
  starting transfers between devices  16.7 us (6%)
  local copies, waits for them, and re-layouts  3.79 us (1%)
    all_to_all x1, blocking collectives, per_device(): state = lax.all_to_all(state.reshape(blocks, block_rows, SIDE), AXES, 0, 0)  105 us
    all_to_all x1, waiting for transfers between devices, per_device(): state = lax.all_to_all(state.reshape(blocks, block_rows, SIDE), AXES, 0, 0)  96.3 us
    pallas_call x2, Pallas kernels, native_layer(): pl.pallas_call(functools.partial(native_kernel, layer, slot), grid=(steps...  18.1 us
    all_to_all x1, starting transfers between devices, per_device(): state = lax.all_to_all(state.reshape(blocks, block_rows, SIDE), AXES, 0, 0)  16.7 us
    max x4, other arithmetic, x_masks(): jnp.maximum(p - 14, 0)  7.74 us
    pallas_call x1, Pallas kernels, middle_layer(): pl.pallas_call(functools.partial(middle_kernel, layer), grid=(rows // 8,)...  6.77 us
  transfers between devices with their start and end apart: 1, of which 1 were waited for; matrix products, arithmetic and copies ran while one was open for 0% of the time, Pallas kernels for 0%

profile of v1, /device:TPU:1, one launch (start us, length us, event | category | flops | bytes accessed | tf_op | source)
XLA Modules:
  0.0 264.1 jit_solution(6473528675636423378)
XLA Ops:
  0.0 2.1 maximum_reduce_fusion.39
  2.1 2.2 compare_reduce_fusion.79
  4.3 1.9 compare_reduce_fusion.78
  6.2 2.2 compare_reduce_fusion.75
  8.4 1.9 maximum_reduce_fusion.29
  10.3 1.9 maximum_reduce_fusion.19
  12.2 1.9 maximum_reduce_fusion.9
  14.1 1.7 compare_reduce_fusion.74
  15.9 1.6 compare_reduce_fusion.77
  17.5 0.8 copy.9.pairs_ref
  18.2 0.3 select_xor_fusion.masks_ref
  18.6 0.0 copy-start.1
  18.6 1.0 copy-done.1
  19.6 8.9 %shard_map.37 = f32[8192,128]{1,0:T(8,128)S(1)} custom-call(s32[3,20,2]{2,1,0:T(8,128)S(1)} %copy.9.pairs_ref, s32[2,64]{1,0:T(2,128)S(1)} %select_xor_fusion.masks_ref, f32[3,2,128,128]{3,2,1,0:T(8,128)S(1)} %copy-done.1, f32[8192,128]{1,0:T(8,128)} %bitcast.10), custom_call_target="tpu_custom_call" | custom-call | flops 2147483648 | bytes 8388608 | tf_op jit(solution)/shard_map/pallas_call | solution.py:104
  28.5 0.0 copy-start
  28.5 2.0 copy-done
  30.5 0.0 copy-start.2
  30.5 16.7 %all-to-all-start = ((f32[256,32,128]{2,1,0:T(8,128)}), f32[256,32,128]{2,1,0:T(8,128)}, u32[]{:S(2)}, u32[]{:S(2)}) async-start(f32[256,32,128]{2,1,0:T(8,128)} %bitcast.7), calls=%async_computation | async-start | bytes 8388608 | tf_op jit(solution)/shard_map/all_to_all | solution.py:211
  47.2 96.3 %all-to-all-done = f32[256,32,128]{2,1,0:T(8,128)} async-done(((f32[256,32,128]{2,1,0:T(8,128)}), f32[256,32,128]{2,1,0:T(8,128)}, u32[]{:S(2)}, u32[]{:S(2)}) %all-to-all-start) | async-done | bytes 4194336 | tf_op jit(solution)/shard_map/all_to_all | solution.py:211
  143.5 0.0 copy-done.2
  143.5 6.8 %shard_map.38 = f32[16,16,32,128]{3,2,1,0:T(8,128)S(1)} custom-call(s32[3,20,2]{2,1,0:T(8,128)S(1)} %copy.9.pairs_ref, s32[1]{0:T(128)} %bitcast.x_ref, f32[3,2,128,128]{3,2,1,0:T(8,128)S(1)} %copy-done.2, f32[16,16,32,128]{3,2,1,0:T(8,128)} %bitcast.3.in_ref), custom_call_target="tpu_custom_call" | custom-call | flops 2147483648 | bytes 8388608 | tf_op jit(solution)/shard_map/pallas_call | solution.py:159
  150.3 104.7 %all_to_all.10 = f32[256,32,128]{2,1,0:T(8,128)S(1)} all-to-all(f32[256,32,128]{2,1,0:T(8,128)S(1)} %bitcast.9), channel_id=1, replica_groups=mesh['qa'=16,'qb'=16] {'qa','qb'}, dimensions={0} | all-to-all | bytes 8388608 | tf_op jit(solution)/shard_map/all_to_all | solution.py:214
  255.0 9.1 %shard_map.39 = f32[8192,128]{1,0:T(8,128)} custom-call(s32[3,20,2]{2,1,0:T(8,128)S(1)} %copy.9.pairs_ref, s32[2,64]{1,0:T(2,128)S(1)} %select_xor_fusion.masks_ref, f32[3,2,128,128]{3,2,1,0:T(8,128)S(1)} %copy-done.2, f32[8192,128]{1,0:T(8,128)S(1)} %bitcast.8), custom_call_target="tpu_custom_call" | custom-call | flops 2147483648 | bytes 8388608 | tf_op jit(solution)/shard_map/pallas_call | solution.py:104
Async XLA Ops:
  18.6 1.0 copy-start.1
  28.5 2.0 copy-start
  30.5 113.0 %copy-start.2 = (f32[3,2,128,128]{3,2,1,0:T(8,128)S(1)}, f32[3,2,128,128]{3,2,1,0:T(8,128)}, u32[]{:S(2)}) copy-start(f32[3,2,128,128]{3,2,1,0:T(8,128)} %gates_ref.5) | copy-start | bytes 1179652
  30.5 113.0 %all-to-all-start = ((f32[256,32,128]{2,1,0:T(8,128)}), f32[256,32,128]{2,1,0:T(8,128)}, u32[]{:S(2)}, u32[]{:S(2)}) async-start(f32[256,32,128]{2,1,0:T(8,128)} %bitcast.7), calls=%async_computation | async-start | bytes 8388608 | tf_op jit(solution)/shard_map/all_to_all | solution.py:211

commit v2 on v1

v2 whole, which is shorter than its diff:
```python
import functools

import jax
import jax.numpy as jnp
from jax import lax
from jax.experimental import pallas as pl
from jax.experimental.pallas import tpu as pltpu
from jax.sharding import PartitionSpec as P

LAYERS = 3
SIDE = 128
CHUNKS = 4
AXES = ("qa", "qb")
VMEM = 48 * 1024 * 1024


def split(value):
    high = value.astype(jnp.bfloat16)
    low = (value - high.astype(jnp.float32)).astype(jnp.bfloat16)
    return high, low


def gate_stack(gate):
    high, low = split(gate)
    high = jnp.concatenate([high, high], 1)
    low = jnp.concatenate([low, low], 1)
    rows = []
    for start in range(0, SIDE, 16):
        rows += [high[start : start + 16], low[start : start + 16]]
    return jnp.concatenate(rows, 0)


def gate_stack_lanes(gate):
    high, low = split(gate)
    return jnp.concatenate(
        [jnp.concatenate([high, high], 1), jnp.concatenate([low, low], 1)], 0
    )


def apply_rows(stack, value):
    high, low = split(value)
    both = jnp.dot(
        stack, jnp.concatenate([high, low], 0), preferred_element_type=jnp.float32
    )
    both = both.reshape(SIDE // 16, 2, 16, value.shape[1])
    return (both[:, 0] + both[:, 1]).reshape(value.shape)


def apply_lanes(stack, value):
    high, low = split(value)
    both = lax.dot_general(
        jnp.concatenate([high, low], 1),
        stack,
        (((1,), (1,)), ((), ())),
        preferred_element_type=jnp.float32,
    )
    return both[:, :SIDE] + both[:, SIDE:]


def sign_of(positions, pairs_ref, layer):
    parity = jnp.zeros(positions.shape, jnp.int32)
    for pair in range(pairs_ref.shape[2]):
        first = jnp.right_shift(positions, pairs_ref[layer, 0, pair])
        second = jnp.right_shift(positions, pairs_ref[layer, 1, pair])
        parity = parity ^ (first & second)
    return 1.0 - 2.0 * (parity & 1).astype(jnp.float32)


def fold_parity(value):
    for shift in (8, 4, 2, 1):
        value = value ^ jnp.right_shift(value, shift)
    return value & 1


def x_masks(x, pairs_ref, layer):
    x_bits = jnp.left_shift(x, 14)
    mask = jnp.zeros(x.shape, jnp.int32)
    for pair in range(pairs_ref.shape[2]):
        p = pairs_ref[layer, 0, pair]
        q = pairs_ref[layer, 1, pair]
        bit_p = jnp.right_shift(x_bits, p) & 1
        bit_q = jnp.right_shift(x_bits, q) & 1
        cross = jnp.left_shift(bit_p, q) ^ jnp.left_shift(bit_q, p)
        mask = mask ^ cross ^ jnp.left_shift(bit_p & bit_q, 20)
    return mask


def sign_table(x, layer, pairs_ref, y_first):
    first = lax.broadcasted_iota(jnp.int32, (SIDE, SIDE), 0)
    last = lax.broadcasted_iota(jnp.int32, (SIDE, SIDE), 1)
    y, z = (first, last) if y_first else (last, first)
    return sign_of(x * (SIDE * SIDE) + y * SIDE + z, pairs_ref, layer)


def native_pair(base, x, source, target, stack_z, stack_y, table, masks):
    low_bits = lax.broadcasted_iota(jnp.int32, (8, SIDE), 0) * SIDE + (
        lax.broadcasted_iota(jnp.int32, (8, SIDE), 1)
    )
    value = apply_lanes(stack_z[...], source[pl.ds(base, 2 * SIDE), :])
    value = apply_rows(stack_y[...], jnp.concatenate([value[:SIDE], value[SIDE:]], 1))
    for half in range(2):
        mask = jnp.broadcast_to(masks[pl.ds(x + half, 1), :], (8, SIDE))
        parity = fold_parity((low_bits & mask) ^ (jnp.right_shift(mask, 20) & 1))
        signs = [1.0 - 2.0 * parity.astype(jnp.float32)]
        for bit in range(4):
            flip = jnp.right_shift(mask, 10 + bit) & 1
            factor = 1.0 - 2.0 * flip.astype(jnp.float32)
            signs = signs + [sign * factor for sign in signs]
        sign = jnp.concatenate(signs, 0) * table[...]
        target[pl.ds(base + half * SIDE, SIDE), :] = (
            value[:, half * SIDE : (half + 1) * SIDE] * sign
        )


def first_kernel(
    pairs_ref, x_ref, gates_ref, in_ref, out_ref, stacks, tables, masks,
    gates, buffer, stack_z, stack_y, table, masks_0, gate_sem, sems,
):
    rows_chunk = in_ref.shape[0] // CHUNKS
    gate_copy = pltpu.make_async_copy(gates_ref, gates, gate_sem)
    gate_copy.start()

    def chunk_copy(chunk):
        part = pl.ds(chunk * rows_chunk, rows_chunk)
        return pltpu.make_async_copy(in_ref.at[part], buffer.at[part], sems.at[chunk])

    for chunk in range(CHUNKS):
        chunk_copy(chunk).start()

    table[...] = sign_table(0, 0, pairs_ref, True)
    tables[0] = sign_table(x_ref[0], 1, pairs_ref, False)
    tables[1] = sign_table(0, 2, pairs_ref, True)
    x = lax.broadcasted_iota(jnp.int32, masks.shape, 0)
    masks_0[...] = x_masks(x, pairs_ref, 0)
    masks[...] = x_masks(x, pairs_ref, 2)
    gate_copy.wait()
    stack_z[...] = gate_stack_lanes(gates[0, 0])
    stack_y[...] = gate_stack(gates[0, 1])
    stacks[0] = gate_stack(gates[1, 0])
    stacks[1] = gate_stack(gates[1, 1])
    stacks[2] = gate_stack_lanes(gates[2, 0])
    stacks[3] = gate_stack(gates[2, 1])

    for chunk in range(CHUNKS):
        chunk_copy(chunk).wait()
        for base in range(chunk * rows_chunk, (chunk + 1) * rows_chunk, 2 * SIDE):
            native_pair(
                base, base // SIDE, buffer, out_ref, stack_z, stack_y, table, masks_0
            )


def last_kernel(stacks, tables, masks, in_ref, out_ref, buffer, sems):
    rows_chunk = in_ref.shape[0] // CHUNKS

    def chunk_copy(chunk):
        part = pl.ds(chunk * rows_chunk, rows_chunk)
        return pltpu.make_async_copy(buffer.at[part], out_ref.at[part], sems.at[chunk])

    for chunk in range(CHUNKS):
        for base in range(chunk * rows_chunk, (chunk + 1) * rows_chunk, 2 * SIDE):
            native_pair(
                base, base // SIDE, in_ref, buffer,
                stacks.at[2], stacks.at[3], tables.at[1], masks,
            )
        chunk_copy(chunk).start()
    for chunk in range(CHUNKS):
        chunk_copy(chunk).wait()


def middle_kernel(stacks, tables, in_ref, out_ref, first, second):
    def square(ref, b, start):
        return ref[:, b, start : start + 8, :].reshape(SIDE, SIDE)

    for part in range(in_ref.shape[2] // 8):
        start = part * 8
        for b in range(0, 16, 2):
            value = jnp.concatenate(
                [square(in_ref, b, start), square(in_ref, b + 1, start)], 1
            )
            value = apply_rows(stacks[1], value)
            first[b] = value[:, :SIDE].T.reshape(16, 8, SIDE)
            first[b + 1] = value[:, SIDE:].T.reshape(16, 8, SIDE)
        for d in range(0, 16, 2):
            value = jnp.concatenate([square(first, d, 0), square(first, d + 1, 0)], 1)
            value = apply_rows(stacks[0], value)
            second[d] = (value[:, :SIDE] * tables[0]).reshape(16, 8, SIDE)
            second[d + 1] = (value[:, SIDE:] * tables[0]).reshape(16, 8, SIDE)
        for b in range(16):
            out_ref[:, b, start : start + 8, :] = square(second, b, 0).T.reshape(
                16, 8, SIDE
            )


WHOLE = pl.BlockSpec(memory_space=pltpu.VMEM)
SCALARS = pl.BlockSpec(memory_space=pltpu.SMEM)
REMOTE = pl.BlockSpec(memory_space=pl.ANY)


def call(kernel, state, in_specs, out_specs, out_shape, scratch_shapes):
    return pl.pallas_call(
        kernel,
        in_specs=in_specs,
        out_specs=out_specs,
        out_shape=out_shape,
        scratch_shapes=scratch_shapes,
        compiler_params=pltpu.CompilerParams(vmem_limit_bytes=VMEM),
        cost_estimate=pl.CostEstimate(
            flops=16 * state.size * SIDE, bytes_accessed=8 * state.size, transcendentals=0
        ),
    )


def first_layer(pairs, x_index, gates, state):
    n_x = state.shape[0] // SIDE
    stack = (2 * SIDE, 2 * SIDE)
    square = (SIDE, SIDE)
    return call(
        first_kernel,
        state,
        [SCALARS, SCALARS, REMOTE, REMOTE],
        [WHOLE] * 4,
        [
            jax.ShapeDtypeStruct(state.shape, jnp.float32),
            jax.ShapeDtypeStruct((4, *stack), jnp.bfloat16),
            jax.ShapeDtypeStruct((2, *square), jnp.float32),
            jax.ShapeDtypeStruct((n_x, SIDE), jnp.int32),
        ],
        [
            pltpu.VMEM(gates.shape, jnp.float32),
            pltpu.VMEM(state.shape, jnp.float32),
            pltpu.VMEM(stack, jnp.bfloat16),
            pltpu.VMEM(stack, jnp.bfloat16),
            pltpu.VMEM(square, jnp.float32),
            pltpu.VMEM((n_x, SIDE), jnp.int32),
            pltpu.SemaphoreType.DMA(()),
            pltpu.SemaphoreType.DMA((CHUNKS,)),
        ],
    )(pairs, x_index, gates, state)


def middle_layer(stacks, tables, state):
    return call(
        middle_kernel,
        state,
        [WHOLE] * 3,
        WHOLE,
        jax.ShapeDtypeStruct(state.shape, jnp.float32),
        [
            pltpu.VMEM((state.shape[1], 16, 8, SIDE), jnp.float32),
            pltpu.VMEM((16, state.shape[1], 8, SIDE), jnp.float32),
        ],
    )(stacks, tables, state)


def last_layer(stacks, tables, masks, state):
    return call(
        last_kernel,
        state,
        [WHOLE] * 4,
        REMOTE,
        jax.ShapeDtypeStruct(state.shape, jnp.float32),
        [
            pltpu.VMEM(state.shape, jnp.float32),
            pltpu.SemaphoreType.DMA((CHUNKS,)),
        ],
    )(stacks, tables, masks, state)


def per_device(amplitudes, gates, cz_pairs):
    total = amplitudes.shape[2]
    n_qa, n_qb = lax.axis_size("qa"), lax.axis_size("qb")
    pairs = cz_pairs.transpose(0, 2, 1)
    state = amplitudes.reshape(total // SIDE, SIDE)
    device = lax.axis_index("qa") * n_qb + lax.axis_index("qb")
    x_index = jnp.right_shift(device, 2).astype(jnp.int32).reshape(1)
    blocks = n_qa * n_qb
    block_rows = total // SIDE // blocks
    state, stacks, tables, masks = first_layer(pairs, x_index, gates, state)
    state = lax.all_to_all(state.reshape(blocks, block_rows, SIDE), AXES, 0, 0)
    state = state.reshape(n_qa, n_qb, block_rows, SIDE)
    state = middle_layer(stacks, tables, state)
    state = lax.all_to_all(state.reshape(blocks, block_rows, SIDE), AXES, 0, 0)
    state = state.reshape(total // SIDE, SIDE)
    state = last_layer(stacks, tables, masks, state)
    return state.reshape(1, 1, total)


def solution(mesh):
    in_specs = (P("qa", "qb", None), P(), P())
    out_specs = P("qa", "qb", None)
    return jax.shard_map(
        per_device, mesh=mesh, in_specs=in_specs, out_specs=out_specs, check_vma=False
    )
```

time: 265 us -> 237 us (0.89)
  blocking collectives: 105 us -> 218 us
  waiting for transfers between devices: 96.3 us -> 0 us
  other arithmetic: 17.7 us -> 0 us
  starting transfers between devices: 16.7 us -> 0 us
  Pallas kernels: 24.8 us -> 17.6 us
    all_to_all x1 -> x2, blocking collectives: 105 us -> 218 us  [per_device(): state = lax.all_to_all(state.reshape(blocks, block_rows, SIDE), AXES, 0, 0)]
    all_to_all x1 -> x0, waiting for transfers between devices: 96.3 us -> none  [per_device(): state = lax.all_to_all(state.reshape(blocks, block_rows, SIDE), AXES, 0, 0)]
    all_to_all x1 -> x0, starting transfers between devices: 16.7 us -> none  [per_device(): state = lax.all_to_all(state.reshape(blocks, block_rows, SIDE), AXES, 0, 0)]
    max x4 -> x0, other arithmetic: 7.74 us -> none  [x_masks(): jnp.maximum(p - 14, 0)]
    pallas_call x3, Pallas kernels: 24.8 us -> 17.6 us  [the longest x1 6.62 us: first_layer(): call(first_kernel, state, [SCALARS, SCALARS, REMOTE, REMOTE], [WHOLE] * 4...]
    lt x3 -> x0, other arithmetic: 6 us -> none  [the longest x2 4.4 us: x_masks(): q < 14]
    ge x2 -> x0, other arithmetic: 3.65 us -> none  [x_masks(): p >= 14]
  transfers between devices with their start and end apart: 1 -> 0, of which waited for: 1 -> 0; matrix products, arithmetic and copies ran while one was open for 0% -> 0% of each run, Pallas kernels for 0% -> 0%
where the time goes in v2:
time: 237 us
  blocking collectives  218 us (92%)
  Pallas kernels  17.6 us (7%)
    all_to_all x2, blocking collectives, per_device(): state = lax.all_to_all(state.reshape(blocks, block_rows, SIDE), AXES, 0, 0)  218 us
    pallas_call x1, Pallas kernels, first_layer(): call(first_kernel, state, [SCALARS, SCALARS, REMOTE, REMOTE], [WHOLE] * 4...  6.62 us
    pallas_call x1, Pallas kernels, middle_layer(): call(middle_kernel, state, [WHOLE] * 3, WHOLE, jax.ShapeDtypeStruct(state...  6.42 us

profile of v2, /device:TPU:1, one launch (start us, length us, event | category | flops | bytes accessed | tf_op | source)
XLA Modules:
  0.0 236.9 jit_solution(4858246498150935951)
XLA Ops:
  0.0 0.0 copy-start
  0.0 1.0 copy-done
  1.0 0.0 copy-start.1
  1.0 0.7 copy-done.1
  1.7 6.6 %shard_map.37 = (f32[8192,128]{1,0:T(8,128)S(1)}, bf16[4,256,256]{2,1,0:T(8,128)(2,1)S(1)}, f32[2,128,128]{2,1,0:T(8,128)S(1)}, s32[64,128]{1,0:T(8,128)S(1)}) custom-call(s32[3,2,20]{2,1,0:T(2,128)S(1)} %bitcast.11, s32[1]{0:T(128)} %bitcast.1.x_ref, f32[3,2,128,128]{3,2,1,0:T(8,128)S(1)} %copy-done, f32[8192,128]{1,0:T(8,128)} %bitcast.13), custom_call_target="tpu_custom_call" | custom-call | flops 2147483648 | bytes 8388608 | tf_op jit(solution)/shard_map/pallas_call | solution.py:217
  8.3 112.8 %all_to_all.10 = f32[256,32,128]{2,1,0:T(8,128)} all-to-all(f32[256,32,128]{2,1,0:T(8,128)S(1)} %bitcast.10), channel_id=1, replica_groups=mesh['qa'=16,'qb'=16] {'qa','qb'}, dimensions={0} | all-to-all | bytes 8388608 | tf_op jit(solution)/shard_map/all_to_all | solution.py:279
  121.1 6.4 %shard_map.38 = f32[16,16,32,128]{3,2,1,0:T(8,128)S(1)} custom-call(bf16[4,256,256]{2,1,0:T(8,128)(2,1)S(1)} %get-tuple-element.9.stacks, f32[2,128,128]{2,1,0:T(8,128)S(1)} %get-tuple-element.10.tables, f32[16,16,32,128]{3,2,1,0:T(8,128)} %bitcast.12), custom_call_target="tpu_custom_call" | custom-call | flops 2147483648 | bytes 8388608 | tf_op jit(solution)/shard_map/pallas_call | solution.py:242
  127.5 104.7 %all_to_all.11 = f32[256,32,128]{2,1,0:T(8,128)S(1)} all-to-all(f32[256,32,128]{2,1,0:T(8,128)S(1)} %bitcast.9), channel_id=1, replica_groups=mesh['qa'=16,'qb'=16] {'qa','qb'}, dimensions={0} | all-to-all | bytes 8388608 | tf_op jit(solution)/shard_map/all_to_all | solution.py:282
  232.3 4.5 %shard_map.39 = f32[8192,128]{1,0:T(8,128)} custom-call(bf16[4,256,256]{2,1,0:T(8,128)(2,1)S(1)} %get-tuple-element.9.stacks, f32[2,128,128]{2,1,0:T(8,128)S(1)} %get-tuple-element.10.tables, s32[64,128]{1,0:T(8,128)S(1)} %get-tuple-element.11.masks, f32[8192,128]{1,0:T(8,128)S(1)} %bitcast.8), custom_call_target="tpu_custom_call" | custom-call | flops 2147483648 | bytes 8388608 | tf_op jit(solution)/shard_map/pallas_call | solution.py:256
Async XLA Ops:
  0.0 1.0 copy-start
  1.0 0.7 copy-start.1

commit v3 on v2

--- a/solution.py
+++ b/solution.py
@@ -9,9 +9,10 @@
 
 LAYERS = 3
 SIDE = 128
-CHUNKS = 4
+IN_CHUNKS = 1
+OUT_CHUNKS = 8
 AXES = ("qa", "qb")
-VMEM = 48 * 1024 * 1024
+MIB = 1024 * 1024
 
 
 def split(value):
@@ -116,7 +117,7 @@
     pairs_ref, x_ref, gates_ref, in_ref, out_ref, stacks, tables, masks,
     gates, buffer, stack_z, stack_y, table, masks_0, gate_sem, sems,
 ):
-    rows_chunk = in_ref.shape[0] // CHUNKS
+    rows_chunk = in_ref.shape[0] // IN_CHUNKS
     gate_copy = pltpu.make_async_copy(gates_ref, gates, gate_sem)
     gate_copy.start()
 
@@ -124,7 +125,7 @@
         part = pl.ds(chunk * rows_chunk, rows_chunk)
         return pltpu.make_async_copy(in_ref.at[part], buffer.at[part], sems.at[chunk])
 
-    for chunk in range(CHUNKS):
+    for chunk in range(IN_CHUNKS):
         chunk_copy(chunk).start()
 
     table[...] = sign_table(0, 0, pairs_ref, True)
@@ -141,7 +142,7 @@
     stacks[2] = gate_stack_lanes(gates[2, 0])
     stacks[3] = gate_stack(gates[2, 1])
 
-    for chunk in range(CHUNKS):
+    for chunk in range(IN_CHUNKS):
         chunk_copy(chunk).wait()
         for base in range(chunk * rows_chunk, (chunk + 1) * rows_chunk, 2 * SIDE):
             native_pair(
@@ -150,20 +151,20 @@
 
 
 def last_kernel(stacks, tables, masks, in_ref, out_ref, buffer, sems):
-    rows_chunk = in_ref.shape[0] // CHUNKS
+    rows_chunk = in_ref.shape[0] // OUT_CHUNKS
 
     def chunk_copy(chunk):
         part = pl.ds(chunk * rows_chunk, rows_chunk)
         return pltpu.make_async_copy(buffer.at[part], out_ref.at[part], sems.at[chunk])
 
-    for chunk in range(CHUNKS):
+    for chunk in range(OUT_CHUNKS):
         for base in range(chunk * rows_chunk, (chunk + 1) * rows_chunk, 2 * SIDE):
             native_pair(
                 base, base // SIDE, in_ref, buffer,
                 stacks.at[2], stacks.at[3], tables.at[1], masks,
             )
         chunk_copy(chunk).start()
-    for chunk in range(CHUNKS):
+    for chunk in range(OUT_CHUNKS):
         chunk_copy(chunk).wait()
 
 
@@ -196,14 +197,14 @@
 REMOTE = pl.BlockSpec(memory_space=pl.ANY)
 
 
-def call(kernel, state, in_specs, out_specs, out_shape, scratch_shapes):
+def call(kernel, state, in_specs, out_specs, out_shape, scratch_shapes, limit):
     return pl.pallas_call(
         kernel,
         in_specs=in_specs,
         out_specs=out_specs,
         out_shape=out_shape,
         scratch_shapes=scratch_shapes,
-        compiler_params=pltpu.CompilerParams(vmem_limit_bytes=VMEM),
+        compiler_params=pltpu.CompilerParams(vmem_limit_bytes=limit),
         cost_estimate=pl.CostEstimate(
             flops=16 * state.size * SIDE, bytes_accessed=8 * state.size, transcendentals=0
         ),
@@ -233,8 +234,9 @@
             pltpu.VMEM(square, jnp.float32),
             pltpu.VMEM((n_x, SIDE), jnp.int32),
             pltpu.SemaphoreType.DMA(()),
-            pltpu.SemaphoreType.DMA((CHUNKS,)),
-        ],
+            pltpu.SemaphoreType.DMA((IN_CHUNKS,)),
+        ],
+        48 * MIB,
     )(pairs, x_index, gates, state)
 
 
@@ -249,6 +251,7 @@
             pltpu.VMEM((state.shape[1], 16, 8, SIDE), jnp.float32),
             pltpu.VMEM((16, state.shape[1], 8, SIDE), jnp.float32),
         ],
+        16 * MIB,
     )(stacks, tables, state)
 
 
@@ -261,8 +264,9 @@
         jax.ShapeDtypeStruct(state.shape, jnp.float32),
         [
             pltpu.VMEM(state.shape, jnp.float32),
-            pltpu.SemaphoreType.DMA((CHUNKS,)),
-        ],
+            pltpu.SemaphoreType.DMA((OUT_CHUNKS,)),
+        ],
+        16 * MIB,
     )(stacks, tables, masks, state)
 
 

time: 237 us -> 235 us (level)
  no operation moved by 1% of the time
where the time goes in v3:
time: 235 us
  blocking collectives  217 us (92%)
  Pallas kernels  15.4 us (7%)
    all_to_all x2, blocking collectives, per_device(): state = lax.all_to_all(state.reshape(blocks, block_rows, SIDE), AXES, 0, 0)  217 us
    pallas_call x1, Pallas kernels, first_layer(): call(first_kernel, state, [SCALARS, SCALARS, REMOTE, REMOTE], [WHOLE] * 4...  6.5 us

profile of v3, /device:TPU:1, one launch (start us, length us, event | category | flops | bytes accessed | tf_op | source)
XLA Modules:
  0.0 234.6 jit_solution(17117359008770692634)
XLA Ops:
  0.0 0.0 copy-start
  0.0 1.0 copy-done
  1.0 0.0 copy-start.1
  1.0 0.7 copy-done.1
  1.7 6.5 %shard_map.37 = (f32[8192,128]{1,0:T(8,128)S(1)}, bf16[4,256,256]{2,1,0:T(8,128)(2,1)S(1)}, f32[2,128,128]{2,1,0:T(8,128)S(1)}, s32[64,128]{1,0:T(8,128)S(1)}) custom-call(s32[3,2,20]{2,1,0:T(2,128)S(1)} %bitcast.12, s32[1]{0:T(128)} %bitcast.1.x_ref, f32[3,2,128,128]{3,2,1,0:T(8,128)S(1)} %copy-done, f32[8192,128]{1,0:T(8,128)} %bitcast.13), custom_call_target="tpu_custom_call" | custom-call | flops 2147483648 | bytes 8388608 | tf_op jit(solution)/shard_map/pallas_call | solution.py:218
  8.2 112.7 %all_to_all.10 = f32[256,32,128]{2,1,0:T(8,128)S(1)} all-to-all(f32[256,32,128]{2,1,0:T(8,128)S(1)} %bitcast.11), channel_id=1, replica_groups=mesh['qa'=16,'qb'=16] {'qa','qb'}, dimensions={0} | all-to-all | bytes 8388608 | tf_op jit(solution)/shard_map/all_to_all | solution.py:283
  120.9 4.3 %shard_map.38 = f32[16,16,32,128]{3,2,1,0:T(8,128)S(1)} custom-call(bf16[4,256,256]{2,1,0:T(8,128)(2,1)S(1)} %get-tuple-element.9.stacks, f32[2,128,128]{2,1,0:T(8,128)S(1)} %get-tuple-element.10.tables, f32[16,16,32,128]{3,2,1,0:T(8,128)S(1)} %bitcast.9), custom_call_target="tpu_custom_call" | custom-call | flops 2147483648 | bytes 8388608 | tf_op jit(solution)/shard_map/pallas_call | solution.py:244
  125.2 104.7 %all_to_all.11 = f32[256,32,128]{2,1,0:T(8,128)S(1)} all-to-all(f32[256,32,128]{2,1,0:T(8,128)S(1)} %bitcast.10), channel_id=1, replica_groups=mesh['qa'=16,'qb'=16] {'qa','qb'}, dimensions={0} | all-to-all | bytes 8388608 | tf_op jit(solution)/shard_map/all_to_all | solution.py:286
  229.9 4.5 %shard_map.39 = f32[8192,128]{1,0:T(8,128)} custom-call(bf16[4,256,256]{2,1,0:T(8,128)(2,1)S(1)} %get-tuple-element.9.stacks, f32[2,128,128]{2,1,0:T(8,128)S(1)} %get-tuple-element.10.tables, s32[64,128]{1,0:T(8,128)S(1)} %get-tuple-element.11.masks, f32[8192,128]{1,0:T(8,128)S(1)} %bitcast.8), custom_call_target="tpu_custom_call" | custom-call | flops 2147483648 | bytes 8388608 | tf_op jit(solution)/shard_map/pallas_call | solution.py:259
Async XLA Ops:
  0.0 1.0 copy-start
  1.0 0.7 copy-start.1

commit v4 on v3

--- a/solution.py
+++ b/solution.py
@@ -9,8 +9,9 @@
 
 LAYERS = 3
 SIDE = 128
-IN_CHUNKS = 1
+IN_CHUNKS = 2
 OUT_CHUNKS = 8
+GROUP = 1024
 AXES = ("qa", "qb")
 MIB = 1024 * 1024
 
@@ -93,11 +94,10 @@
     return sign_of(x * (SIDE * SIDE) + y * SIDE + z, pairs_ref, layer)
 
 
-def native_pair(base, x, source, target, stack_z, stack_y, table, masks):
+def native_pair(base, x, value, target, stack_y, table, masks):
     low_bits = lax.broadcasted_iota(jnp.int32, (8, SIDE), 0) * SIDE + (
         lax.broadcasted_iota(jnp.int32, (8, SIDE), 1)
     )
-    value = apply_lanes(stack_z[...], source[pl.ds(base, 2 * SIDE), :])
     value = apply_rows(stack_y[...], jnp.concatenate([value[:SIDE], value[SIDE:]], 1))
     for half in range(2):
         mask = jnp.broadcast_to(masks[pl.ds(x + half, 1), :], (8, SIDE))
@@ -113,10 +113,31 @@
         )
 
 
+def native_y(start, count, target, stack_y, table, masks):
+    for base in range(start, start + count, 2 * SIDE):
+        native_pair(
+            base, base // SIDE, target[pl.ds(base, 2 * SIDE), :],
+            target, stack_y, table, masks,
+        )
+
+
+def native_rows(start, count, source, target, stack_z, stack_y, table, masks):
+    for group in range(start, start + count, GROUP):
+        target[pl.ds(group, GROUP), :] = apply_lanes(stack_z[...], source[pl.ds(group, GROUP), :])
+    for group in range(start, start + count, GROUP):
+        for base in range(group, group + GROUP, 2 * SIDE):
+            native_pair(
+                base, base // SIDE, target[pl.ds(base, 2 * SIDE), :],
+                target, stack_y, table, masks,
+            )
+
+
 def first_kernel(
     pairs_ref, x_ref, gates_ref, in_ref, out_ref, stacks, tables, masks,
-    gates, buffer, stack_z, stack_y, table, masks_0, gate_sem, sems,
+    gates, buffer, stack_z, stack_y, table, masks_0, pairs, pair_sem, gate_sem, sems,
 ):
+    pair_copy = pltpu.make_async_copy(pairs_ref, pairs, pair_sem)
+    pair_copy.start()
     rows_chunk = in_ref.shape[0] // IN_CHUNKS
     gate_copy = pltpu.make_async_copy(gates_ref, gates, gate_sem)
     gate_copy.start()
@@ -128,12 +149,13 @@
     for chunk in range(IN_CHUNKS):
         chunk_copy(chunk).start()
 
-    table[...] = sign_table(0, 0, pairs_ref, True)
-    tables[0] = sign_table(x_ref[0], 1, pairs_ref, False)
-    tables[1] = sign_table(0, 2, pairs_ref, True)
+    pair_copy.wait()
+    table[...] = sign_table(0, 0, pairs, True)
+    tables[0] = sign_table(x_ref[0], 1, pairs, False)
+    tables[1] = sign_table(0, 2, pairs, True)
     x = lax.broadcasted_iota(jnp.int32, masks.shape, 0)
-    masks_0[...] = x_masks(x, pairs_ref, 0)
-    masks[...] = x_masks(x, pairs_ref, 2)
+    masks_0[...] = x_masks(x, pairs, 0)
+    masks[...] = x_masks(x, pairs, 2)
     gate_copy.wait()
     stack_z[...] = gate_stack_lanes(gates[0, 0])
     stack_y[...] = gate_stack(gates[0, 1])
@@ -144,10 +166,10 @@
 
     for chunk in range(IN_CHUNKS):
         chunk_copy(chunk).wait()
-        for base in range(chunk * rows_chunk, (chunk + 1) * rows_chunk, 2 * SIDE):
-            native_pair(
-                base, base // SIDE, buffer, out_ref, stack_z, stack_y, table, masks_0
-            )
+        for group in range(chunk * rows_chunk, (chunk + 1) * rows_chunk, GROUP):
+            part = pl.ds(group, GROUP)
+            out_ref[part, :] = apply_lanes(stack_z[...], buffer[part, :])
+    native_y(0, in_ref.shape[0], out_ref, stack_y, table, masks_0)
 
 
 def last_kernel(stacks, tables, masks, in_ref, out_ref, buffer, sems):
@@ -158,11 +180,10 @@
         return pltpu.make_async_copy(buffer.at[part], out_ref.at[part], sems.at[chunk])
 
     for chunk in range(OUT_CHUNKS):
-        for base in range(chunk * rows_chunk, (chunk + 1) * rows_chunk, 2 * SIDE):
-            native_pair(
-                base, base // SIDE, in_ref, buffer,
-                stacks.at[2], stacks.at[3], tables.at[1], masks,
-            )
+        native_rows(
+            chunk * rows_chunk, rows_chunk, in_ref, buffer,
+            stacks.at[2], stacks.at[3], tables.at[1], masks,
+        )
         chunk_copy(chunk).start()
     for chunk in range(OUT_CHUNKS):
         chunk_copy(chunk).wait()
@@ -211,6 +232,10 @@
     )
 
 
+def in_hbm(value):
+    return pltpu.with_memory_space_constraint(value, pltpu.HBM)
+
+
 def first_layer(pairs, x_index, gates, state):
     n_x = state.shape[0] // SIDE
     stack = (2 * SIDE, 2 * SIDE)
@@ -218,7 +243,7 @@
     return call(
         first_kernel,
         state,
-        [SCALARS, SCALARS, REMOTE, REMOTE],
+        [REMOTE, SCALARS, REMOTE, REMOTE],
         [WHOLE] * 4,
         [
             jax.ShapeDtypeStruct(state.shape, jnp.float32),
@@ -233,11 +258,13 @@
             pltpu.VMEM(stack, jnp.bfloat16),
             pltpu.VMEM(square, jnp.float32),
             pltpu.VMEM((n_x, SIDE), jnp.int32),
+            pltpu.SMEM(pairs.shape, jnp.int32),
+            pltpu.SemaphoreType.DMA(()),
             pltpu.SemaphoreType.DMA(()),
             pltpu.SemaphoreType.DMA((IN_CHUNKS,)),
         ],
         48 * MIB,
-    )(pairs, x_index, gates, state)
+    )(in_hbm(pairs), x_index, in_hbm(gates), state)
 
 
 def middle_layer(stacks, tables, state):

time: 235 us -> 231 us (0.983)
  no operation moved by 1% of the time
where the time goes in v4:
time: 231 us
  blocking collectives  217 us (94%)
  Pallas kernels  13.7 us (6%)
    all_to_all x2, blocking collectives, per_device(): state = lax.all_to_all(state.reshape(blocks, block_rows, SIDE), AXES, 0, 0)  217 us
    pallas_call x1, Pallas kernels, first_layer(): call(first_kernel, state, [REMOTE, SCALARS, REMOTE, REMOTE], [WHOLE] * 4,...  5.03 us

profile of v4, /device:TPU:1, one launch (start us, length us, event | category | flops | bytes accessed | tf_op | source)
XLA Modules:
  0.0 231.3 jit_solution(15366223469332757766)
XLA Ops:
  0.0 5.0 %shard_map.37 = (f32[8192,128]{1,0:T(8,128)S(1)}, bf16[4,256,256]{2,1,0:T(8,128)(2,1)S(1)}, f32[2,128,128]{2,1,0:T(8,128)S(1)}, s32[64,128]{1,0:T(8,128)S(1)}) custom-call(s32[3,2,20]{2,1,0:T(2,128)} %bitcast.13, s32[1]{0:T(128)} %bitcast.1.x_ref, f32[3,2,128,128]{3,2,1,0:T(8,128)} %gates_ref.1, f32[8192,128]{1,0:T(8,128)} %bitcast.12), custom_call_target="tpu_custom_call" | custom-call | flops 2147483648 | bytes 8388608 | tf_op jit(solution)/shard_map/pallas_call | solution.py:243
  5.0 112.7 %all_to_all.10 = f32[256,32,128]{2,1,0:T(8,128)S(1)} all-to-all(f32[256,32,128]{2,1,0:T(8,128)S(1)} %bitcast.11), channel_id=1, replica_groups=mesh['qa'=16,'qb'=16] {'qa','qb'}, dimensions={0} | all-to-all | bytes 8388608 | tf_op jit(solution)/shard_map/all_to_all | solution.py:310
  117.7 4.3 %shard_map.38 = f32[16,16,32,128]{3,2,1,0:T(8,128)S(1)} custom-call(bf16[4,256,256]{2,1,0:T(8,128)(2,1)S(1)} %get-tuple-element.9.stacks, f32[2,128,128]{2,1,0:T(8,128)S(1)} %get-tuple-element.10.tables, f32[16,16,32,128]{3,2,1,0:T(8,128)S(1)} %bitcast.9), custom_call_target="tpu_custom_call" | custom-call | flops 2147483648 | bytes 8388608 | tf_op jit(solution)/shard_map/pallas_call | solution.py:271
  122.0 104.7 %all_to_all.11 = f32[256,32,128]{2,1,0:T(8,128)S(1)} all-to-all(f32[256,32,128]{2,1,0:T(8,128)S(1)} %bitcast.10), channel_id=1, replica_groups=mesh['qa'=16,'qb'=16] {'qa','qb'}, dimensions={0} | all-to-all | bytes 8388608 | tf_op jit(solution)/shard_map/all_to_all | solution.py:313
  226.7 4.4 %shard_map.39 = f32[8192,128]{1,0:T(8,128)} custom-call(bf16[4,256,256]{2,1,0:T(8,128)(2,1)S(1)} %get-tuple-element.9.stacks, f32[2,128,128]{2,1,0:T(8,128)S(1)} %get-tuple-element.10.tables, s32[64,128]{1,0:T(8,128)S(1)} %get-tuple-element.11.masks, f32[8192,128]{1,0:T(8,128)S(1)} %bitcast.8), custom_call_target="tpu_custom_call" | custom-call | flops 2147483648 | bytes 8388608 | tf_op jit(solution)/shard_map/pallas_call | solution.py:286

commit v5 on v4

--- a/solution.py
+++ b/solution.py
@@ -7,7 +7,6 @@
 from jax.experimental.pallas import tpu as pltpu
 from jax.sharding import PartitionSpec as P
 
-LAYERS = 3
 SIDE = 128
 IN_CHUNKS = 2
 OUT_CHUNKS = 8
@@ -119,17 +118,6 @@
             base, base // SIDE, target[pl.ds(base, 2 * SIDE), :],
             target, stack_y, table, masks,
         )
-
-
-def native_rows(start, count, source, target, stack_z, stack_y, table, masks):
-    for group in range(start, start + count, GROUP):
-        target[pl.ds(group, GROUP), :] = apply_lanes(stack_z[...], source[pl.ds(group, GROUP), :])
-    for group in range(start, start + count, GROUP):
-        for base in range(group, group + GROUP, 2 * SIDE):
-            native_pair(
-                base, base // SIDE, target[pl.ds(base, 2 * SIDE), :],
-                target, stack_y, table, masks,
-            )
 
 
 def first_kernel(
@@ -179,12 +167,21 @@
         part = pl.ds(chunk * rows_chunk, rows_chunk)
         return pltpu.make_async_copy(buffer.at[part], out_ref.at[part], sems.at[chunk])
 
-    for chunk in range(OUT_CHUNKS):
-        native_rows(
-            chunk * rows_chunk, rows_chunk, in_ref, buffer,
-            stacks.at[2], stacks.at[3], tables.at[1], masks,
-        )
-        chunk_copy(chunk).start()
+    def gate_z(base):
+        part = pl.ds(base, 2 * SIDE)
+        buffer[part, :] = apply_lanes(stacks[2], in_ref[part, :])
+
+    def gate_y(base):
+        native_y(base, 2 * SIDE, buffer, stacks.at[3], tables.at[1], masks)
+
+    for chunk in range(OUT_CHUNKS + 1):
+        for base in range(chunk * rows_chunk, (chunk + 1) * rows_chunk, 2 * SIDE):
+            if chunk < OUT_CHUNKS:
+                gate_z(base)
+            if chunk > 0:
+                gate_y(base - rows_chunk)
+        if chunk > 0:
+            chunk_copy(chunk - 1).start()
     for chunk in range(OUT_CHUNKS):
         chunk_copy(chunk).wait()
 
@@ -193,24 +190,37 @@
     def square(ref, b, start):
         return ref[:, b, start : start + 8, :].reshape(SIDE, SIDE)
 
-    for part in range(in_ref.shape[2] // 8):
-        start = part * 8
+    parts = in_ref.shape[2] // 8
+
+    def gate_y(part, b):
+        value = jnp.concatenate(
+            [square(in_ref, b, part * 8), square(in_ref, b + 1, part * 8)], 1
+        )
+        value = apply_rows(stacks[1], value)
+        slot = first.at[part % 2]
+        slot[b] = value[:, :SIDE].T.reshape(16, 8, SIDE)
+        slot[b + 1] = value[:, SIDE:].T.reshape(16, 8, SIDE)
+
+    def gate_z(part, d):
+        source, target = first.at[part % 2], second.at[part % 2]
+        value = jnp.concatenate([square(source, d, 0), square(source, d + 1, 0)], 1)
+        value = apply_rows(stacks[0], value)
+        target[d] = (value[:, :SIDE] * tables[0]).reshape(16, 8, SIDE)
+        target[d + 1] = (value[:, SIDE:] * tables[0]).reshape(16, 8, SIDE)
+
+    def turn(part, b):
+        for one in (b, b + 1):
+            value = square(second.at[part % 2], one, 0).T.reshape(16, 8, SIDE)
+            out_ref[:, one, part * 8 : part * 8 + 8, :] = value
+
+    for part in range(parts + 2):
         for b in range(0, 16, 2):
-            value = jnp.concatenate(
-                [square(in_ref, b, start), square(in_ref, b + 1, start)], 1
-            )
-            value = apply_rows(stacks[1], value)
-            first[b] = value[:, :SIDE].T.reshape(16, 8, SIDE)
-            first[b + 1] = value[:, SIDE:].T.reshape(16, 8, SIDE)
-        for d in range(0, 16, 2):
-            value = jnp.concatenate([square(first, d, 0), square(first, d + 1, 0)], 1)
-            value = apply_rows(stacks[0], value)
-            second[d] = (value[:, :SIDE] * tables[0]).reshape(16, 8, SIDE)
-            second[d + 1] = (value[:, SIDE:] * tables[0]).reshape(16, 8, SIDE)
-        for b in range(16):
-            out_ref[:, b, start : start + 8, :] = square(second, b, 0).T.reshape(
-                16, 8, SIDE
-            )
+            if part < parts:
+                gate_y(part, b)
+            if 0 <= part - 1 < parts:
+                gate_z(part - 1, b)
+            if 0 <= part - 2 < parts:
+                turn(part - 2, b)
 
 
 WHOLE = pl.BlockSpec(memory_space=pltpu.VMEM)
@@ -275,8 +285,8 @@
         WHOLE,
         jax.ShapeDtypeStruct(state.shape, jnp.float32),
         [
-            pltpu.VMEM((state.shape[1], 16, 8, SIDE), jnp.float32),
-            pltpu.VMEM((16, state.shape[1], 8, SIDE), jnp.float32),
+            pltpu.VMEM((2, state.shape[1], 16, 8, SIDE), jnp.float32),
+            pltpu.VMEM((2, 16, state.shape[1], 8, SIDE), jnp.float32),
         ],
         16 * MIB,
     )(stacks, tables, state)

time: 231 us -> 231 us (level)
  no operation moved by 1% of the time
where the time goes in v5:
time: 231 us; the launch traced here: 230 us
  blocking collectives  217 us (94%)
  Pallas kernels  12.8 us (6%)
    all_to_all x2, blocking collectives, per_device(): state = lax.all_to_all(state.reshape(blocks, block_rows, SIDE), AXES, 0, 0)  217 us
    pallas_call x1, Pallas kernels, first_layer(): call(first_kernel, state, [REMOTE, SCALARS, REMOTE, REMOTE], [WHOLE] * 4,...  5.03 us

profile of v5, /device:TPU:1, one launch (start us, length us, event | category | flops | bytes accessed | tf_op | source)
XLA Modules:
  0.0 230.4 jit_solution(8823664477432155332)
XLA Ops:
  0.0 5.0 %shard_map.37 = (f32[8192,128]{1,0:T(8,128)S(1)}, bf16[4,256,256]{2,1,0:T(8,128)(2,1)S(1)}, f32[2,128,128]{2,1,0:T(8,128)S(1)}, s32[64,128]{1,0:T(8,128)S(1)}) custom-call(s32[3,2,20]{2,1,0:T(2,128)} %bitcast.13, s32[1]{0:T(128)} %bitcast.1.x_ref, f32[3,2,128,128]{3,2,1,0:T(8,128)} %gates_ref.1, f32[8192,128]{1,0:T(8,128)} %bitcast.12), custom_call_target="tpu_custom_call" | custom-call | flops 2147483648 | bytes 8388608 | tf_op jit(solution)/shard_map/pallas_call | solution.py:253
  5.0 112.7 %all_to_all.10 = f32[256,32,128]{2,1,0:T(8,128)S(1)} all-to-all(f32[256,32,128]{2,1,0:T(8,128)S(1)} %bitcast.11), channel_id=1, replica_groups=mesh['qa'=16,'qb'=16] {'qa','qb'}, dimensions={0} | all-to-all | bytes 8388608 | tf_op jit(solution)/shard_map/all_to_all | solution.py:320
  117.7 3.7 %shard_map.38 = f32[16,16,32,128]{3,2,1,0:T(8,128)S(1)} custom-call(bf16[4,256,256]{2,1,0:T(8,128)(2,1)S(1)} %get-tuple-element.9.stacks, f32[2,128,128]{2,1,0:T(8,128)S(1)} %get-tuple-element.10.tables, f32[16,16,32,128]{3,2,1,0:T(8,128)S(1)} %bitcast.9), custom_call_target="tpu_custom_call" | custom-call | flops 2147483648 | bytes 8388608 | tf_op jit(solution)/shard_map/pallas_call | solution.py:281
  121.4 104.7 %all_to_all.11 = f32[256,32,128]{2,1,0:T(8,128)S(1)} all-to-all(f32[256,32,128]{2,1,0:T(8,128)S(1)} %bitcast.10), channel_id=1, replica_groups=mesh['qa'=16,'qb'=16] {'qa','qb'}, dimensions={0} | all-to-all | bytes 8388608 | tf_op jit(solution)/shard_map/all_to_all | solution.py:323
  226.1 4.1 %shard_map.39 = f32[8192,128]{1,0:T(8,128)} custom-call(bf16[4,256,256]{2,1,0:T(8,128)(2,1)S(1)} %get-tuple-element.9.stacks, f32[2,128,128]{2,1,0:T(8,128)S(1)} %get-tuple-element.10.tables, s32[64,128]{1,0:T(8,128)S(1)} %get-tuple-element.11.masks, f32[8192,128]{1,0:T(8,128)S(1)} %bitcast.8), custom_call_target="tpu_custom_call" | custom-call | flops 2147483648 | bytes 8388608 | tf_op jit(solution)/shard_map/pallas_call | solution.py:296

commit v6 on v5

--- a/solution.py
+++ b/solution.py
@@ -11,6 +11,7 @@
 IN_CHUNKS = 2
 OUT_CHUNKS = 8
 GROUP = 1024
+TURNED_EVERY = 3
 AXES = ("qa", "qb")
 MIB = 1024 * 1024
 
@@ -93,11 +94,17 @@
     return sign_of(x * (SIDE * SIDE) + y * SIDE + z, pairs_ref, layer)
 
 
-def native_pair(base, x, value, target, stack_y, table, masks):
+def native_pair(base, x, value, target, stack_y, turned, table, masks):
     low_bits = lax.broadcasted_iota(jnp.int32, (8, SIDE), 0) * SIDE + (
         lax.broadcasted_iota(jnp.int32, (8, SIDE), 1)
     )
-    value = apply_rows(stack_y[...], jnp.concatenate([value[:SIDE], value[SIDE:]], 1))
+    if turned is None:
+        value = jnp.concatenate([value[:SIDE], value[SIDE:]], 1)
+        value = apply_rows(stack_y[...], value)
+    else:
+        value = jnp.concatenate([value[:SIDE].T, value[SIDE:].T], 0)
+        value = apply_lanes(turned[...], value)
+        value = jnp.concatenate([value[:SIDE].T, value[SIDE:].T], 1)
     for half in range(2):
         mask = jnp.broadcast_to(masks[pl.ds(x + half, 1), :], (8, SIDE))
         parity = fold_parity((low_bits & mask) ^ (jnp.right_shift(mask, 20) & 1))
@@ -112,17 +119,17 @@
         )
 
 
-def native_y(start, count, target, stack_y, table, masks):
+def native_y(start, count, target, stack_y, turned, every, table, masks):
     for base in range(start, start + count, 2 * SIDE):
         native_pair(
-            base, base // SIDE, target[pl.ds(base, 2 * SIDE), :],
-            target, stack_y, table, masks,
+            base, base // SIDE, target[pl.ds(base, 2 * SIDE), :], target, stack_y,
+            turned if base // (2 * SIDE) % every == every - 1 else None, table, masks,
         )
 
 
 def first_kernel(
     pairs_ref, x_ref, gates_ref, in_ref, out_ref, stacks, tables, masks,
-    gates, buffer, stack_z, stack_y, table, masks_0, pairs, pair_sem, gate_sem, sems,
+    gates, buffer, stack_z, stack_y, turned, table, masks_0, pairs, pair_sem, gate_sem, sems,
 ):
     pair_copy = pltpu.make_async_copy(pairs_ref, pairs, pair_sem)
     pair_copy.start()
@@ -147,17 +154,20 @@
     gate_copy.wait()
     stack_z[...] = gate_stack_lanes(gates[0, 0])
     stack_y[...] = gate_stack(gates[0, 1])
+    turned[...] = gate_stack_lanes(gates[0, 1])
     stacks[0] = gate_stack(gates[1, 0])
-    stacks[1] = gate_stack(gates[1, 1])
+    stacks[1] = gate_stack_lanes(gates[1, 1])
     stacks[2] = gate_stack_lanes(gates[2, 0])
-    stacks[3] = gate_stack(gates[2, 1])
+    stacks[3] = gate_stack_lanes(gates[2, 1])
 
     for chunk in range(IN_CHUNKS):
         chunk_copy(chunk).wait()
         for group in range(chunk * rows_chunk, (chunk + 1) * rows_chunk, GROUP):
             part = pl.ds(group, GROUP)
             out_ref[part, :] = apply_lanes(stack_z[...], buffer[part, :])
-    native_y(0, in_ref.shape[0], out_ref, stack_y, table, masks_0)
+    native_y(
+        0, in_ref.shape[0], out_ref, stack_y, turned, TURNED_EVERY, table, masks_0
+    )
 
 
 def last_kernel(stacks, tables, masks, in_ref, out_ref, buffer, sems):
@@ -172,7 +182,10 @@
         buffer[part, :] = apply_lanes(stacks[2], in_ref[part, :])
 
     def gate_y(base):
-        native_y(base, 2 * SIDE, buffer, stacks.at[3], tables.at[1], masks)
+        native_y(
+            base, 2 * SIDE, buffer, None, stacks.at[3], 1,
+            tables.at[1], masks,
+        )
 
     for chunk in range(OUT_CHUNKS + 1):
         for base in range(chunk * rows_chunk, (chunk + 1) * rows_chunk, 2 * SIDE):
@@ -193,13 +206,13 @@
     parts = in_ref.shape[2] // 8
 
     def gate_y(part, b):
+        slot = first.at[part % 2]
         value = jnp.concatenate(
-            [square(in_ref, b, part * 8), square(in_ref, b + 1, part * 8)], 1
+            [square(in_ref, b, part * 8).T, square(in_ref, b + 1, part * 8).T], 0
         )
-        value = apply_rows(stacks[1], value)
-        slot = first.at[part % 2]
-        slot[b] = value[:, :SIDE].T.reshape(16, 8, SIDE)
-        slot[b + 1] = value[:, SIDE:].T.reshape(16, 8, SIDE)
+        value = apply_lanes(stacks[1], value)
+        slot[b] = value[:SIDE].reshape(16, 8, SIDE)
+        slot[b + 1] = value[SIDE:].reshape(16, 8, SIDE)
 
     def gate_z(part, d):
         source, target = first.at[part % 2], second.at[part % 2]
@@ -266,6 +279,7 @@
             pltpu.VMEM(state.shape, jnp.float32),
             pltpu.VMEM(stack, jnp.bfloat16),
             pltpu.VMEM(stack, jnp.bfloat16),
+            pltpu.VMEM(stack, jnp.bfloat16),
             pltpu.VMEM(square, jnp.float32),
             pltpu.VMEM((n_x, SIDE), jnp.int32),
             pltpu.SMEM(pairs.shape, jnp.int32),

time: 231 us -> 230 us (level)
  no operation moved by 1% of the time
where the time goes in v6:
time: 230 us
  blocking collectives  217 us (94%)
  Pallas kernels  12.3 us (5%)
    all_to_all x2, blocking collectives, per_device(): state = lax.all_to_all(state.reshape(blocks, block_rows, SIDE), AXES, 0, 0)  217 us
    pallas_call x1, Pallas kernels, first_layer(): call(first_kernel, state, [REMOTE, SCALARS, REMOTE, REMOTE], [WHOLE] * 4,...  4.92 us

profile of v6, /device:TPU:1, one launch (start us, length us, event | category | flops | bytes accessed | tf_op | source)
XLA Modules:
  0.0 229.9 jit_solution(520372300791693046)
XLA Ops:
  0.0 4.9 %shard_map.37 = (f32[8192,128]{1,0:T(8,128)S(1)}, bf16[4,256,256]{2,1,0:T(8,128)(2,1)S(1)}, f32[2,128,128]{2,1,0:T(8,128)S(1)}, s32[64,128]{1,0:T(8,128)S(1)}) custom-call(s32[3,2,20]{2,1,0:T(2,128)} %bitcast.13, s32[1]{0:T(128)} %bitcast.1.x_ref, f32[3,2,128,128]{3,2,1,0:T(8,128)} %gates_ref.1, f32[8192,128]{1,0:T(8,128)} %bitcast.12), custom_call_target="tpu_custom_call" | custom-call | flops 2147483648 | bytes 8388608 | tf_op jit(solution)/shard_map/pallas_call | solution.py:266
  4.9 112.7 %all_to_all.10 = f32[256,32,128]{2,1,0:T(8,128)S(1)} all-to-all(f32[256,32,128]{2,1,0:T(8,128)S(1)} %bitcast.11), channel_id=1, replica_groups=mesh['qa'=16,'qb'=16] {'qa','qb'}, dimensions={0} | all-to-all | bytes 8388608 | tf_op jit(solution)/shard_map/all_to_all | solution.py:334
  117.6 3.6 %shard_map.38 = f32[16,16,32,128]{3,2,1,0:T(8,128)S(1)} custom-call(bf16[4,256,256]{2,1,0:T(8,128)(2,1)S(1)} %get-tuple-element.9.stacks, f32[2,128,128]{2,1,0:T(8,128)S(1)} %get-tuple-element.10.tables, f32[16,16,32,128]{3,2,1,0:T(8,128)S(1)} %bitcast.9), custom_call_target="tpu_custom_call" | custom-call | flops 2147483648 | bytes 8388608 | tf_op jit(solution)/shard_map/pallas_call | solution.py:295
  121.2 104.7 %all_to_all.11 = f32[256,32,128]{2,1,0:T(8,128)S(1)} all-to-all(f32[256,32,128]{2,1,0:T(8,128)S(1)} %bitcast.10), channel_id=1, replica_groups=mesh['qa'=16,'qb'=16] {'qa','qb'}, dimensions={0} | all-to-all | bytes 8388608 | tf_op jit(solution)/shard_map/all_to_all | solution.py:337
  225.9 3.8 %shard_map.39 = f32[8192,128]{1,0:T(8,128)} custom-call(bf16[4,256,256]{2,1,0:T(8,128)(2,1)S(1)} %get-tuple-element.9.stacks, f32[2,128,128]{2,1,0:T(8,128)S(1)} %get-tuple-element.10.tables, s32[64,128]{1,0:T(8,128)S(1)} %get-tuple-element.11.masks, f32[8192,128]{1,0:T(8,128)S(1)} %bitcast.8), custom_call_target="tpu_custom_call" | custom-call | flops 2147483648 | bytes 8388608 | tf_op jit(solution)/shard_map/pallas_call | solution.py:310
